TPU v7x, 32 devices: a whole 2x2x4 slice. The times are simulated.
32 devices in a mesh: gx: 8 (over z, y), gz: 4 (over x, core).
Axes of the slice: x: 2, y: 2, z: 4, core: 2. Of those that a mesh axis runs over, the one named last changes fastest.
Arguments:
- thermal_undercool: float32 [16, 384, 512], P(None, 'gx', 'gz'), may hold values from -1 to 1
- mixture_alloying: float32 [16, 384, 512], P(None, 'gx', 'gz'), may hold values from 0.5 to 1.5
- fluid_fraction: float32 [16, 384, 512], P(None, 'gx', 'gz'), may hold values from 0.05 to 0.95
- kozeny_factor: float32 [16, 384, 512], P(None, 'gx', 'gz'), may hold values from 0.5 to 2
- state_marker: int32 [16, 384, 512], P(None, 'gx', 'gz'), may hold values from 0 to 2
Outputs:
- pressure: float32 [16, 384, 512], P(None, 'gx', 'gz')
- solute_out: float32 [16, 384, 512], P(None, 'gx', 'gz')
Inputs may be any that keep to these rules, and one draw needn't show every extreme that they name: `state_marker`: 0 marks a mushy cell, 1 a liquid one, 2 a solid one.
All inputs are finite; a program needn't handle non-finite values.
Results may differ from a plain program's by a relative error of at most 0.0003.
Values sent between devices are 32-bit elements; how exact they have to be, the bound alone decides.
A program may use at most 64 MiB of HBM per device.

v0:
```python
import jax
import jax.numpy as jnp
from jax import lax
from jax.sharding import PartitionSpec as P

STEPS = 4
SWEEPS = 3


solute_rate = 0.5


def entering(value, axis, join, neutral):
    count, mine = (lax.axis_size(axis), lax.axis_index(axis))
    pieces = lax.all_gather(value, axis)
    subtotal = jnp.full_like(value, 0) + jnp.asarray(neutral, value.dtype)

    def step(position, subtotal):
        longer = join(subtotal, pieces[position])
        return jnp.where(position < mine, longer, subtotal)

    return lax.fori_loop(0, count - 1, step, subtotal)


def with_halo(cells, sides, width):
    for axis, dim in sides:
        count = lax.axis_size(axis)
        ends = count - 1
        head = lax.slice_in_dim(cells, 0, width, axis=dim)
        tail = lax.slice_in_dim(cells, cells.shape[dim] - width, cells.shape[dim], axis=dim)
        cells = jnp.concatenate(
            [
                lax.ppermute(tail, axis, [(i, (i + 1) % count) for i in range(ends)]),
                cells,
                lax.ppermute(head, axis, [((i + 1) % count, i) for i in range(ends)]),
            ],
            axis=dim,
        )
    return cells


def neighbours_of(extended):
    center = extended[:, 1:-1, 1:-1]
    padded = jnp.pad(center, ((1, 1), (0, 0), (0, 0)))
    return (
        center,
        [
            extended[:, 2:, 1:-1],
            extended[:, :-2, 1:-1],
            padded[2:],
            padded[:-2],
            extended[:, 1:-1, 2:],
            extended[:, 1:-1, :-2],
        ],
    )


def face_terms(perm_ext, density_ext, gravity):
    perm_mid, perm_near = neighbours_of(perm_ext)
    density_mid, density_near = neighbours_of(density_ext)
    conductance = [0.5 * (perm_mid + other) for other in perm_near]
    diagonal = conductance[0]
    for face_index in range(1, 6):
        diagonal = diagonal + conductance[face_index]
    lift_down = gravity * 0.5 * (density_mid + density_near[4])
    lift_up = -(gravity * 0.5 * (density_mid + density_near[5]))
    return (conductance, diagonal, lift_down, lift_up)


def jacobi_sweep(pressure_ext, coupling, forcing_amount):
    conductance, diagonal, lift_down, lift_up = coupling
    _, pressure_near = neighbours_of(pressure_ext)
    numerator = forcing_amount - conductance[4] * lift_down - conductance[5] * lift_up
    for face_index in range(6):
        numerator = numerator + conductance[face_index] * pressure_near[face_index]
    return numerator / diagonal


def solute_update(pressure_ext, conc_ext, coupling, molten_state):
    conductance, _, lift_down, lift_up = coupling
    pressure_mid, pressure_near = neighbours_of(pressure_ext)
    conc_mid, conc_near = neighbours_of(conc_ext)
    change = jnp.zeros_like(conc_mid)
    for face_index in range(6):
        driving = pressure_mid - pressure_near[face_index]
        if face_index == 4:
            driving = driving + lift_down
        if face_index == 5:
            driving = driving + lift_up
        flow_out = conductance[face_index] * driving
        change = (
            change
            + jnp.maximum(flow_out, 0.0) * conc_mid
            + jnp.minimum(flow_out, 0.0) * conc_near[face_index]
        )
    return conc_mid - solute_rate * change / (molten_state + 0.1)


def add_pair(earlier, later):
    return earlier + later


def on_device(thermal_undercool, mixture_alloying, fluid_fraction, kozeny_factor, state_marker):
    layered_slabs, vertical_strips, elevation_rows = thermal_undercool.shape
    cells_x = vertical_strips * lax.axis_size("gx")
    cells_z = elevation_rows * lax.axis_size("gz")
    gravity = 4.0 / cells_z
    molten_state = jnp.where(
        state_marker == 1, 1.0, jnp.where(state_marker == 2, 0.0, fluid_fraction)
    )
    darcian_conductivity = kozeny_factor * (
        molten_state**3 / ((1.0 - molten_state) ** 2 + 0.25) + 0.02
    )
    forcing_amount = 2.0 * molten_state * (1.0 - molten_state) * thermal_undercool
    upper_ones = (
        lax.broadcasted_iota(jnp.int32, (elevation_rows, elevation_rows), 0)
        < lax.broadcasted_iota(jnp.int32, (elevation_rows, elevation_rows), 1)
    ).astype(jnp.float32)
    alloying_content = mixture_alloying
    pressure = jnp.zeros_like(mixture_alloying)
    static_pressure = with_halo(
        jnp.stack([darcian_conductivity, thermal_undercool]), (("gx", 2), ("gz", 3)), 1
    )
    perm_ext = static_pressure[0]
    temp_ext = static_pressure[1]
    x_global = lax.axis_index("gx") * vertical_strips + jnp.arange(vertical_strips + 2 * 1) - 1
    z_global = lax.axis_index("gz") * elevation_rows + jnp.arange(elevation_rows + 2 * 1) - 1
    inside_one = (
        ((x_global >= 0) & (x_global < cells_x))[:, None]
        & ((z_global >= 0) & (z_global < cells_z))[None, :]
    )[None]
    for time_step in range(STEPS):
        molten_mass_per_volume = 1.0 + 0.2 * alloying_content - 0.3 * thermal_undercool
        partial_value = jnp.dot(
            molten_mass_per_volume.reshape(layered_slabs * vertical_strips, elevation_rows),
            upper_ones,
            precision=lax.Precision.HIGHEST,
        ).reshape(layered_slabs, vertical_strips, elevation_rows)
        totals = jnp.sum(molten_mass_per_volume, axis=2)
        offset = entering(totals, "gz", add_pair, jnp.zeros_like(totals))
        pressure = gravity * (offset[:, :, None] + partial_value + 0.5 * molten_mass_per_volume)
        conc_ext = with_halo(alloying_content, (("gx", 1), ("gz", 2)), 1)
        density_ext = jnp.where(inside_one, 1.0 + 0.2 * conc_ext - 0.3 * temp_ext, 0.0)
        coupling = face_terms(perm_ext, density_ext, gravity)
        for sweep_index in range(SWEEPS + 1):
            pressure_ext = with_halo(pressure, (("gx", 1), ("gz", 2)), 1)
            if sweep_index < SWEEPS:
                pressure = jacobi_sweep(pressure_ext, coupling, forcing_amount)
        alloying_content = solute_update(pressure_ext, conc_ext, coupling, molten_state)
    return (pressure, alloying_content)


def solution(mesh):
    placed = (
        P(None, "gx", "gz"),
        P(None, "gx", "gz"),
        P(None, "gx", "gz"),
        P(None, "gx", "gz"),
        P(None, "gx", "gz"),
    )
    return jax.shard_map(
        on_device,
        mesh=mesh,
        in_specs=placed,
        out_specs=(P(None, "gx", "gz"), P(None, "gx", "gz")),
        check_vma=False,
    )
```

profile of v0, /device:TPU:26, one launch (start us, length us, event | category | flops | bytes accessed | tf_op | source)
XLA Modules:
  0.0 470.7 jit_solution(14855917229890414974)
XLA Ops:
  11.5 4.2 collective-permute-start.5
  15.9 5.2 %all-gather = f32[64,48]{1,0:T(8,128)S(1)} all-gather(f32[16,48]{1,0:T(8,128)S(1)} %fusion.337), channel_id=2, replica_groups=mesh['gx'=8,'gz'=4] {'gz'}, dimensions={0}, use_global_device_ids=true | all-gather | bytes 15360 | tf_op jit(solution)/shard_map/all_gather | solution.py:15
  23.7 3.9 collective-permute-start.9
  85.6 3.8 collective-permute-start.17
  123.9 3.8 collective-permute-done.23
  127.7 6.0 %fusion.338 = (f32[16,48]{1,0:T(8,128)S(1)}, f32[16,48,128]{2,1,0:T(8,128)S(1)}) fusion(f32[16,48,128]{2,1,0:T(8,128)S(1)} %copy-done, f32[16,48,128]{2,1,0:T(8,128)} %param.14, f32[16,48,128]{2,1,0:T(8,128)S(1)} %get-tuple-element.436, f32[16,1,128]{2,1,0:T(1,128)} %copy-done.26, f32[16,1,128]{2,1,0:T(1,128)} %copy-done.25, ...), kind=kLoop, calls=%fused_computation.600 | loop fusion | flops 7765248 | bytes 5553664 | tf_op jit(solution)/shard_map/reduce_sum | solution.py:139
  133.7 5.6 %all-gather.1 = f32[64,48]{1,0:T(8,128)} all-gather(f32[16,48]{1,0:T(8,128)S(1)} %get-tuple-element.424), channel_id=3, replica_groups=mesh['gx'=8,'gz'=4] {'gz'}, dimensions={0}, use_global_device_ids=true | all-gather | bytes 15360 | tf_op jit(solution)/shard_map/all_gather | solution.py:15
  139.4 3.9 while.57
  146.5 4.6 collective-permute-start.25
  153.1 3.9 collective-permute-start.29
  159.4 3.8 collective-permute-start.27
  169.6 4.3 collective-permute-done.30
  193.6 3.8 collective-permute-done.35
  200.0 3.8 collective-permute-start.37
  238.2 3.8 collective-permute-done.43
  242.0 6.0 %fusion.339 = (f32[16,48]{1,0:T(8,128)S(1)}, f32[16,48,128]{2,1,0:T(8,128)}) fusion(f32[16,48,128]{2,1,0:T(8,128)S(1)} %copy-done, f32[16,48,128]{2,1,0:T(8,128)S(1)} %get-tuple-element.425, f32[16,48,128]{2,1,0:T(8,128)S(1)} %get-tuple-element.436, f32[16,1,128]{2,1,0:T(1,128)} %copy-done.29, f32[16,1,128]{2,1,0:T(1,128)} %copy-done.27, ...), kind=kLoop, calls=%fused_computation.601 | loop fusion | flops 7765248 | bytes 5553664 | tf_op jit(solution)/shard_map/reduce_sum | solution.py:139
  248.0 5.8 %all-gather.2 = f32[64,48]{1,0:T(8,128)} all-gather(f32[16,48]{1,0:T(8,128)S(1)} %get-tuple-element.420), channel_id=4, replica_groups=mesh['gx'=8,'gz'=4] {'gz'}, dimensions={0}, use_global_device_ids=true | all-gather | bytes 15360 | tf_op jit(solution)/shard_map/all_gather | solution.py:15
  253.8 3.9 while.58
  262.3 4.6 collective-permute-start.45
  268.8 3.9 collective-permute-start.49
  285.3 4.3 collective-permute-done.50
  309.1 3.8 collective-permute-done.55
  315.5 3.9 collective-permute-start.57
  330.1 3.8 collective-permute-done.59
  336.5 3.9 collective-permute-start.61
  352.8 3.8 collective-permute-done.63
  356.7 5.4 %fusion.340 = (f32[16,48]{1,0:T(8,128)S(1)}, f32[16,48,128]{2,1,0:T(8,128)S(1)}) fusion(f32[16,48,128]{2,1,0:T(8,128)S(1)} %copy-done, f32[16,48,128]{2,1,0:T(8,128)S(1)} %copy-done.8, f32[16,48,128]{2,1,0:T(8,128)S(1)} %get-tuple-element.436, f32[16,1,128]{2,1,0:T(1,128)} %copy-done.30, f32[16,1,128]{2,1,0:T(1,128)} %copy-done.28, ...), kind=kLoop, calls=%fused_computation.602 | loop fusion | flops 7765248 | bytes 5553664 | tf_op jit(solution)/shard_map/reduce_sum | solution.py:139
  369.6 5.2 %all-gather.3 = f32[64,48]{1,0:T(8,128)S(1)} all-gather(f32[16,48]{1,0:T(8,128)S(1)} %get-tuple-element.416), channel_id=5, replica_groups=mesh['gx'=8,'gz'=4] {'gz'}, dimensions={0}, use_global_device_ids=true | all-gather | bytes 15360 | tf_op jit(solution)/shard_map/all_gather | solution.py:15
  381.5 3.9 collective-permute-start.69
  398.9 4.4 collective-permute-done.70
  429.1 3.9 collective-permute-start.77
  450.1 3.9 collective-permute-start.81
  (341 shorter events, 340.0 us)
Async XLA Ops:
  2.2 32.2 %collective-permute-start = (f32[2,16,1,128]{3,2,1,0:T(1,128)S(1)}, f32[2,16,1,128]{3,2,1,0:T(1,128)S(1)}, u32[]{:S(2)}, u32[]{:S(2)}) collective-permute-start(f32[2,16,1,128]{3,2,1,0:T(1,128)S(1)} %get-tuple-element.439), channel_id=1, source_target_pairs={{0,4},{4,8},{8,12},{12,16},{16,20},{20,24},{24,28},{1,5},{5,9},{9,... | collective-permute-start | bytes 49160 | tf_op jit(solution)/shard_map/ppermute | solution.py:33
  5.6 28.8 %collective-permute-start.1 = (f32[2,16,1,128]{3,2,1,0:T(1,128)S(1)}, f32[2,16,1,128]{3,2,1,0:T(1,128)S(1)}, u32[]{:S(2)}, u32[]{:S(2)}) collective-permute-start(f32[2,16,1,128]{3,2,1,0:T(1,128)S(1)} %get-tuple-element.440), channel_id=1, source_target_pairs={{4,0},{8,4},{12,8},{16,12},{20,16},{24,20},{28,24},{5,1},{9,5},{13... | collective-permute-start | bytes 49160 | tf_op jit(solution)/shard_map/ppermute | solution.py:35
  9.0 14.7 %collective-permute-start.4 = (f32[16,1,128]{2,1,0:T(1,128)S(1)}, f32[16,1,128]{2,1,0:T(1,128)S(1)}, u32[]{:S(2)}, u32[]{:S(2)}) collective-permute-start(f32[16,1,128]{2,1,0:T(1,128)S(1)} %get-tuple-element.517), channel_id=1, source_target_pairs={{0,4},{4,8},{8,12},{12,16},{16,20},{20,24},{24,28},{1,5},{5,9},{9,... | collective-permute-start | bytes 24584 | tf_op jit(solution)/shard_map/ppermute | solution.py:33
  11.5 16.1 %collective-permute-start.5 = (f32[16,1,128]{2,1,0:T(1,128)S(1)}, f32[16,1,128]{2,1,0:T(1,128)S(1)}, u32[]{:S(2)}, u32[]{:S(2)}) collective-permute-start(f32[16,1,128]{2,1,0:T(1,128)S(1)} %get-tuple-element.518), channel_id=1, source_target_pairs={{4,0},{8,4},{12,8},{16,12},{20,16},{24,20},{28,24},{5,1},{9,5},{13... | collective-permute-start | bytes 24584 | tf_op jit(solution)/shard_map/ppermute | solution.py:35
  23.7 10.6 %collective-permute-start.9 = (f32[16,1,128]{2,1,0:T(1,128)S(1)}, f32[16,1,128]{2,1,0:T(1,128)S(1)}, u32[]{:S(2)}, u32[]{:S(2)}) collective-permute-start(f32[16,1,128]{2,1,0:T(1,128)S(1)} %get-tuple-element.519), channel_id=1, source_target_pairs={{0,4},{4,8},{8,12},{12,16},{16,20},{20,24},{24,28},{1,5},{5,9},{9,... | collective-permute-start | bytes 24584 | tf_op jit(solution)/shard_map/ppermute | solution.py:33
  28.7 26.0 %collective-permute-start.6 = (f32[16,50,1]{2,1,0:T(8,128)}, f32[16,50,1]{2,1,0:T(8,128)}, u32[]{:S(2)}, u32[]{:S(2)}) collective-permute-start(f32[16,50,1]{2,1,0:T(8,128)} %get-tuple-element.477), channel_id=1, source_target_pairs={{0,1},{1,2},{2,3},{4,5},{5,6},{6,7},{8,9},{9,10},{10,11},{12,13},{... | collective-permute-start | bytes 9608 | tf_op jit(solution)/shard_map/ppermute | solution.py:33
  30.6 24.1 %collective-permute-start.7 = (f32[16,50,1]{2,1,0:T(8,128)}, f32[16,50,1]{2,1,0:T(8,128)}, u32[]{:S(2)}, u32[]{:S(2)}) collective-permute-start(f32[16,50,1]{2,1,0:T(8,128)} %get-tuple-element.478), channel_id=1, source_target_pairs={{1,0},{2,1},{3,2},{5,4},{6,5},{7,6},{9,8},{10,9},{11,10},{13,12},{... | collective-permute-start | bytes 9608 | tf_op jit(solution)/shard_map/ppermute | solution.py:35
  37.6 10.1 %collective-permute-start.3 = (f32[2,16,50,1]{2,1,3,0:T(8,128)S(1)}, f32[2,16,50,1]{2,1,3,0:T(8,128)S(1)}, u32[]{:S(2)}, u32[]{:S(2)}) collective-permute-start(f32[2,16,50,1]{2,1,3,0:T(8,128)S(1)} %copy.8), channel_id=1, source_target_pairs={{1,0},{2,1},{3,2},{5,4},{6,5},{7,6},{9,8},{10,9},{11,10},{13,12},{... | collective-permute-start | bytes 19208 | tf_op jit(solution)/shard_map/ppermute | solution.py:35
  41.0 9.9 %collective-permute-start.2 = (f32[2,16,50,1]{2,1,3,0:T(8,128)S(1)}, f32[2,16,50,1]{2,1,3,0:T(8,128)S(1)}, u32[]{:S(2)}, u32[]{:S(2)}) collective-permute-start(f32[2,16,50,1]{2,1,3,0:T(8,128)S(1)} %copy.7), channel_id=1, source_target_pairs={{0,1},{1,2},{2,3},{4,5},{5,6},{6,7},{8,9},{9,10},{10,11},{12,13},{... | collective-permute-start | bytes 19208 | tf_op jit(solution)/shard_map/ppermute | solution.py:33
  44.5 12.8 %collective-permute-start.10 = (f32[16,50,1]{2,1,0:T(8,128)}, f32[16,50,1]{2,1,0:T(8,128)}, u32[]{:S(2)}, u32[]{:S(2)}) collective-permute-start(f32[16,50,1]{2,1,0:T(8,128)} %get-tuple-element.479), channel_id=1, source_target_pairs={{1,0},{2,1},{3,2},{5,4},{6,5},{7,6},{9,8},{10,9},{11,10},{13,12},{... | collective-permute-start | bytes 9608 | tf_op jit(solution)/shard_map/ppermute | solution.py:35
  47.7 10.1 %collective-permute-start.11 = (f32[16,50,1]{2,1,0:T(8,128)}, f32[16,50,1]{2,1,0:T(8,128)}, u32[]{:S(2)}, u32[]{:S(2)}) collective-permute-start(f32[16,50,1]{2,1,0:T(8,128)} %get-tuple-element.480), channel_id=1, source_target_pairs={{0,1},{1,2},{2,3},{4,5},{5,6},{6,7},{8,9},{9,10},{10,11},{12,13},{... | collective-permute-start | bytes 9608 | tf_op jit(solution)/shard_map/ppermute | solution.py:33
  117.6 10.1 %collective-permute-start.23 = (f32[16,50,1]{2,1,0:T(8,128)}, f32[16,50,1]{2,1,0:T(8,128)}, u32[]{:S(2)}, u32[]{:S(2)}) collective-permute-start(f32[16,50,1]{2,1,0:T(8,128)} %get-tuple-element.472), channel_id=1, source_target_pairs={{0,1},{1,2},{2,3},{4,5},{5,6},{6,7},{8,9},{9,10},{10,11},{12,13},{... | collective-permute-start | bytes 9608 | tf_op jit(solution)/shard_map/ppermute | solution.py:33
  144.4 12.6 %collective-permute-start.24 = (f32[16,1,128]{2,1,0:T(1,128)S(1)}, f32[16,1,128]{2,1,0:T(1,128)S(1)}, u32[]{:S(2)}, u32[]{:S(2)}) collective-permute-start(f32[16,1,128]{2,1,0:T(1,128)S(1)} %get-tuple-element.509), channel_id=1, source_target_pairs={{0,4},{4,8},{8,12},{12,16},{16,20},{20,24},{24,28},{1,5},{5,9},{9,... | collective-permute-start | bytes 24584 | tf_op jit(solution)/shard_map/ppermute | solution.py:33
  146.5 10.5 %collective-permute-start.25 = (f32[16,1,128]{2,1,0:T(1,128)S(1)}, f32[16,1,128]{2,1,0:T(1,128)S(1)}, u32[]{:S(2)}, u32[]{:S(2)}) collective-permute-start(f32[16,1,128]{2,1,0:T(1,128)S(1)} %get-tuple-element.510), channel_id=1, source_target_pairs={{4,0},{8,4},{12,8},{16,12},{20,16},{24,20},{28,24},{5,1},{9,5},{13... | collective-permute-start | bytes 24584 | tf_op jit(solution)/shard_map/ppermute | solution.py:35
  151.2 12.0 %collective-permute-start.28 = (f32[16,1,128]{2,1,0:T(1,128)S(1)}, f32[16,1,128]{2,1,0:T(1,128)S(1)}, u32[]{:S(2)}, u32[]{:S(2)}) collective-permute-start(f32[16,1,128]{2,1,0:T(1,128)S(1)} %get-tuple-element.508), channel_id=1, source_target_pairs={{4,0},{8,4},{12,8},{16,12},{20,16},{24,20},{28,24},{5,1},{9,5},{13... | collective-permute-start | bytes 24584 | tf_op jit(solution)/shard_map/ppermute | solution.py:35
  153.1 10.1 %collective-permute-start.29 = (f32[16,1,128]{2,1,0:T(1,128)S(1)}, f32[16,1,128]{2,1,0:T(1,128)S(1)}, u32[]{:S(2)}, u32[]{:S(2)}) collective-permute-start(f32[16,1,128]{2,1,0:T(1,128)S(1)} %get-tuple-element.507), channel_id=1, source_target_pairs={{0,4},{4,8},{8,12},{12,16},{16,20},{20,24},{24,28},{1,5},{5,9},{9,... | collective-permute-start | bytes 24584 | tf_op jit(solution)/shard_map/ppermute | solution.py:33
  157.3 10.7 %collective-permute-start.26 = (f32[16,50,1]{2,1,0:T(8,128)S(1)}, f32[16,50,1]{2,1,0:T(8,128)S(1)}, u32[]{:S(2)}, u32[]{:S(2)}) collective-permute-start(f32[16,50,1]{2,1,0:T(8,128)S(1)} %get-tuple-element.470), channel_id=1, source_target_pairs={{0,1},{1,2},{2,3},{4,5},{5,6},{6,7},{8,9},{9,10},{10,11},{12,13},{... | collective-permute-start | bytes 9608 | tf_op jit(solution)/shard_map/ppermute | solution.py:33
  163.5 10.4 %collective-permute-start.30 = (f32[16,50,1]{2,1,0:T(8,128)S(1)}, f32[16,50,1]{2,1,0:T(8,128)S(1)}, u32[]{:S(2)}, u32[]{:S(2)}) collective-permute-start(f32[16,50,1]{2,1,0:T(8,128)S(1)} %get-tuple-element.467), channel_id=1, source_target_pairs={{1,0},{2,1},{3,2},{5,4},{6,5},{7,6},{9,8},{10,9},{11,10},{13,12},{... | collective-permute-start | bytes 9608 | tf_op jit(solution)/shard_map/ppermute | solution.py:35
  231.9 10.1 %collective-permute-start.43 = (f32[16,50,1]{2,1,0:T(8,128)}, f32[16,50,1]{2,1,0:T(8,128)}, u32[]{:S(2)}, u32[]{:S(2)}) collective-permute-start(f32[16,50,1]{2,1,0:T(8,128)} %get-tuple-element.462), channel_id=1, source_target_pairs={{0,1},{1,2},{2,3},{4,5},{5,6},{6,7},{8,9},{9,10},{10,11},{12,13},{... | collective-permute-start | bytes 9608 | tf_op jit(solution)/shard_map/ppermute | solution.py:33
  260.1 12.6 %collective-permute-start.44 = (f32[16,1,128]{2,1,0:T(1,128)S(1)}, f32[16,1,128]{2,1,0:T(1,128)S(1)}, u32[]{:S(2)}, u32[]{:S(2)}) collective-permute-start(f32[16,1,128]{2,1,0:T(1,128)S(1)} %get-tuple-element.499), channel_id=1, source_target_pairs={{0,4},{4,8},{8,12},{12,16},{16,20},{20,24},{24,28},{1,5},{5,9},{9,... | collective-permute-start | bytes 24584 | tf_op jit(solution)/shard_map/ppermute | solution.py:33
  262.3 10.5 %collective-permute-start.45 = (f32[16,1,128]{2,1,0:T(1,128)S(1)}, f32[16,1,128]{2,1,0:T(1,128)S(1)}, u32[]{:S(2)}, u32[]{:S(2)}) collective-permute-start(f32[16,1,128]{2,1,0:T(1,128)S(1)} %get-tuple-element.500), channel_id=1, source_target_pairs={{4,0},{8,4},{12,8},{16,12},{20,16},{24,20},{28,24},{5,1},{9,5},{13... | collective-permute-start | bytes 24584 | tf_op jit(solution)/shard_map/ppermute | solution.py:35
  266.9 11.9 %collective-permute-start.48 = (f32[16,1,128]{2,1,0:T(1,128)S(1)}, f32[16,1,128]{2,1,0:T(1,128)S(1)}, u32[]{:S(2)}, u32[]{:S(2)}) collective-permute-start(f32[16,1,128]{2,1,0:T(1,128)S(1)} %get-tuple-element.498), channel_id=1, source_target_pairs={{4,0},{8,4},{12,8},{16,12},{20,16},{24,20},{28,24},{5,1},{9,5},{13... | collective-permute-start | bytes 24584 | tf_op jit(solution)/shard_map/ppermute | solution.py:35
  268.8 10.0 %collective-permute-start.49 = (f32[16,1,128]{2,1,0:T(1,128)S(1)}, f32[16,1,128]{2,1,0:T(1,128)S(1)}, u32[]{:S(2)}, u32[]{:S(2)}) collective-permute-start(f32[16,1,128]{2,1,0:T(1,128)S(1)} %get-tuple-element.497), channel_id=1, source_target_pairs={{0,4},{4,8},{8,12},{12,16},{16,20},{20,24},{24,28},{1,5},{5,9},{9,... | collective-permute-start | bytes 24584 | tf_op jit(solution)/shard_map/ppermute | solution.py:33
  273.1 10.5 %collective-permute-start.46 = (f32[16,50,1]{2,1,0:T(8,128)S(1)}, f32[16,50,1]{2,1,0:T(8,128)S(1)}, u32[]{:S(2)}, u32[]{:S(2)}) collective-permute-start(f32[16,50,1]{2,1,0:T(8,128)S(1)} %get-tuple-element.460), channel_id=1, source_target_pairs={{0,1},{1,2},{2,3},{4,5},{5,6},{6,7},{8,9},{9,10},{10,11},{12,13},{... | collective-permute-start | bytes 9608 | tf_op jit(solution)/shard_map/ppermute | solution.py:33
  279.1 10.6 %collective-permute-start.50 = (f32[16,50,1]{2,1,0:T(8,128)S(1)}, f32[16,50,1]{2,1,0:T(8,128)S(1)}, u32[]{:S(2)}, u32[]{:S(2)}) collective-permute-start(f32[16,50,1]{2,1,0:T(8,128)S(1)} %get-tuple-element.457), channel_id=1, source_target_pairs={{1,0},{2,1},{3,2},{5,4},{6,5},{7,6},{9,8},{10,9},{11,10},{13,12},{... | collective-permute-start | bytes 9608 | tf_op jit(solution)/shard_map/ppermute | solution.py:35
  346.5 10.1 %collective-permute-start.63 = (f32[16,50,1]{2,1,0:T(8,128)}, f32[16,50,1]{2,1,0:T(8,128)}, u32[]{:S(2)}, u32[]{:S(2)}) collective-permute-start(f32[16,50,1]{2,1,0:T(8,128)} %get-tuple-element.452), channel_id=1, source_target_pairs={{0,1},{1,2},{2,3},{4,5},{5,6},{6,7},{8,9},{9,10},{10,11},{12,13},{... | collective-permute-start | bytes 9608 | tf_op jit(solution)/shard_map/ppermute | solution.py:33
  362.8 22.6 %collective-permute-start.64 = (f32[16,1,128]{2,1,0:T(1,128)S(1)}, f32[16,1,128]{2,1,0:T(1,128)S(1)}, u32[]{:S(2)}, u32[]{:S(2)}) collective-permute-start(f32[16,1,128]{2,1,0:T(1,128)S(1)} %get-tuple-element.487), channel_id=1, source_target_pairs={{0,4},{4,8},{8,12},{12,16},{16,20},{20,24},{24,28},{1,5},{5,9},{9,... | collective-permute-start | bytes 24584 | tf_op jit(solution)/shard_map/ppermute | solution.py:33
  365.8 19.6 %collective-permute-start.65 = (f32[16,1,128]{2,1,0:T(1,128)S(1)}, f32[16,1,128]{2,1,0:T(1,128)S(1)}, u32[]{:S(2)}, u32[]{:S(2)}) collective-permute-start(f32[16,1,128]{2,1,0:T(1,128)S(1)} %get-tuple-element.488), channel_id=1, source_target_pairs={{4,0},{8,4},{12,8},{16,12},{20,16},{24,20},{28,24},{5,1},{9,5},{13... | collective-permute-start | bytes 24584 | tf_op jit(solution)/shard_map/ppermute | solution.py:35
  379.5 12.8 %collective-permute-start.68 = (f32[16,1,128]{2,1,0:T(1,128)S(1)}, f32[16,1,128]{2,1,0:T(1,128)S(1)}, u32[]{:S(2)}, u32[]{:S(2)}) collective-permute-start(f32[16,1,128]{2,1,0:T(1,128)S(1)} %get-tuple-element.490), channel_id=1, source_target_pairs={{4,0},{8,4},{12,8},{16,12},{20,16},{24,20},{28,24},{5,1},{9,5},{13... | collective-permute-start | bytes 24584 | tf_op jit(solution)/shard_map/ppermute | solution.py:35
  381.5 10.9 %collective-permute-start.69 = (f32[16,1,128]{2,1,0:T(1,128)S(1)}, f32[16,1,128]{2,1,0:T(1,128)S(1)}, u32[]{:S(2)}, u32[]{:S(2)}) collective-permute-start(f32[16,1,128]{2,1,0:T(1,128)S(1)} %get-tuple-element.489), channel_id=1, source_target_pairs={{0,4},{4,8},{8,12},{12,16},{16,20},{20,24},{24,28},{1,5},{5,9},{9,... | collective-permute-start | bytes 24584 | tf_op jit(solution)/shard_map/ppermute | solution.py:33
  386.7 10.5 %collective-permute-start.66 = (f32[16,50,1]{2,1,0:T(8,128)S(1)}, f32[16,50,1]{2,1,0:T(8,128)S(1)}, u32[]{:S(2)}, u32[]{:S(2)}) collective-permute-start(f32[16,50,1]{2,1,0:T(8,128)S(1)} %get-tuple-element.447), channel_id=1, source_target_pairs={{0,1},{1,2},{2,3},{4,5},{5,6},{6,7},{8,9},{9,10},{10,11},{12,13},{... | collective-permute-start | bytes 9608 | tf_op jit(solution)/shard_map/ppermute | solution.py:33
  392.7 10.6 %collective-permute-start.70 = (f32[16,50,1]{2,1,0:T(8,128)S(1)}, f32[16,50,1]{2,1,0:T(8,128)S(1)}, u32[]{:S(2)}, u32[]{:S(2)}) collective-permute-start(f32[16,50,1]{2,1,0:T(8,128)S(1)} %get-tuple-element.449), channel_id=1, source_target_pairs={{1,0},{2,1},{3,2},{5,4},{6,5},{7,6},{9,8},{10,9},{11,10},{13,12},{... | collective-permute-start | bytes 9608 | tf_op jit(solution)/shard_map/ppermute | solution.py:35
  (93 other events, 757.9 us)
where the time goes:
time: 474 us; the launch traced here: 471 us
  starting transfers between devices  227 us (48%)
  waiting for transfers between devices  144 us (30%)
  other arithmetic  51 us (11%)
  blocking collectives  21.8 us (5%)
  local copies, waits for them, and re-layouts  19.9 us (4%)
    ppermute x42, starting transfers between devices, with_halo(): lax.ppermute(tail, axis, [(i, (i + 1) % count) for i in range(ends)])  121 us
    ppermute x42, starting transfers between devices, with_halo(): lax.ppermute(head, axis, [((i + 1) % count, i) for i in range(ends)])  106 us
    ppermute x42, waiting for transfers between devices, with_halo(): lax.ppermute(tail, axis, [(i, (i + 1) % count) for i in range(ends)])  85.9 us
    ppermute x42, waiting for transfers between devices, with_halo(): lax.ppermute(head, axis, [((i + 1) % count, i) for i in range(ends)])  57.7 us
    all_gather x4, blocking collectives, entering(): pieces = lax.all_gather(value, axis)  21.8 us
    reduce_sum x4, other arithmetic, on_device(): totals = jnp.sum(molten_mass_per_volume, axis=2)  17.6 us
    select_n x12, other arithmetic, step(): return jnp.where(position < mine, longer, subtotal)  11.1 us
    div x12, other arithmetic, jacobi_sweep(): return numerator / diagonal  10.2 us
  transfers between devices with their start and end apart: 84, of which 46 were waited for; matrix products, arithmetic and copies ran while one was open for 5% of the time, Pallas kernels for 0%

commit v1 on v0

v1 whole, which is shorter than its diff:
```python
import functools

import jax
import jax.numpy as jnp
from jax import lax
from jax.experimental import pallas as pl
from jax.experimental.pallas import tpu as pltpu
from jax.sharding import PartitionSpec as P

STEPS = 4
SWEEPS = 3
W = SWEEPS + 1
SOLUTE_RATE = 0.5
MESH = pl.DeviceIdType.MESH
UNROLL = 2

LO = 8


def kernel(nx, nz, *refs):
    it = iter(refs)
    t_in, c_in, f_in, k_in, m_in, p_out, c_out = [next(it) for _ in range(7)]
    perm, temp, ca, cb, pa, pb = [next(it) for _ in range(6)]
    axp, axm, ayp, aym, azp, azm, srcn = [next(it) for _ in range(7)]
    cxp, cyp, czp, czm, rl, bb, ld, lu = [next(it) for _ in range(8)]
    hf = next(it)
    off = next(it)
    xs, xr, rs, rr, es, er, ls, lr, fs, fr = [next(it) for _ in range(10)]
    sxs, sxr, szs, szr, ses, ser = [next(it) for _ in range(6)]
    send_sem, recv_sem, st_send, st_recv = [next(it) for _ in range(4)]

    ny, n, lanes = t_in.shape
    wide = n + 2 * W
    hi_row = LO + wide
    mid = LO + W
    gravity = 4.0 / (nz * lanes)
    half = 0.5 * gravity
    ix, iz = lax.axis_index("gx"), lax.axis_index("gz")
    f32, bf16 = jnp.float32, jnp.bfloat16

    CONC, PERM, TEMP, SRC, PH, BH, AXP, AXM, AYP, AYM, AZP, AZM, SRCN, RHO = range(14)

    def inside(dx, dz):
        return (ix + dx >= 0) & (ix + dx < nx) & (iz + dz >= 0) & (iz + dz < nz)

    partners = [(dx, dz) for dz in range(-1, nz) for dx in (-1, 0, 1) if (dx, dz) != (0, 0)]

    def step_copies(s):
        out = []
        for dx, dz in partners:
            a, b = (1, 0) if dx > 0 else (0, 1)
            if dz == 0:
                src, dst = xs.at[s, a], xr.at[s, b]
            elif dz > 0 and dx == 0:
                src, dst = rs.at[s], rr.at[s, dz - 1]
            elif dz > 0:
                src, dst = es.at[s, a], er.at[s, b, dz - 1]
            elif dx == 0:
                src, dst = ls.at[s], lr.at[s]
            else:
                src, dst = fs.at[s, a], fr.at[s, b]
            m = len(out)
            out.append((dx, dz, pltpu.make_async_remote_copy(
                src_ref=src, dst_ref=dst, send_sem=send_sem.at[s, m], recv_sem=recv_sem.at[s, m],
                device_id={"gx": ix + dx, "gz": iz + dz}, device_id_type=MESH)))
        return out

    def static_copies():
        out = []
        for dx, dz in partners:
            if dz > 1:
                continue
            a, b = (1, 0) if dx > 0 else (0, 1)
            if dz == 0:
                src, dst = sxs.at[a], sxr.at[b]
            elif dx == 0:
                src, dst = szs, szr.at[0 if dz > 0 else 1]
            else:
                src, dst = ses.at[a], ser.at[b, 0 if dz > 0 else 1]
            m = len(out)
            out.append((dx, dz, pltpu.make_async_remote_copy(
                src_ref=src, dst_ref=dst, send_sem=st_send.at[m], recv_sem=st_recv.at[m],
                device_id={"gx": ix + dx, "gz": iz + dz}, device_id_type=MESH)))
        return out

    def start(copies):
        for dx, dz, c in copies:
            pl.when(inside(dx, dz))(c.start)

    def arrive(copies):
        for dx, dz, c in copies:
            pl.when(inside(-dx, -dz))(c.wait_recv)

    def sent(copies):
        for dx, dz, c in copies:
            pl.when(inside(dx, dz))(c.wait_send)

    for ref in (xr, rr, er, lr, fr, sxr, szr, ser):
        ref[...] = jnp.zeros_like(ref)
    barrier = pltpu.get_barrier_semaphore()
    count = 0
    for dx, dz in partners:
        @pl.when(inside(-dx, -dz))
        def _(dx=dx, dz=dz):
            pl.semaphore_signal(barrier, inc=1, device_id={"gx": ix - dx, "gz": iz - dz}, device_id_type=MESH)
        count = count + inside(dx, dz).astype(jnp.int32)

    def yloop(body, init):
        def group(g, carry):
            for u in range(UNROLL):
                carry = body(g * UNROLL + u, carry)
            return carry
        return lax.fori_loop(0, ny // UNROLL, group, init)

    lane_n = lax.broadcasted_iota(jnp.int32, (n, lanes), 1)
    lane_w = lax.broadcasted_iota(jnp.int32, (wide, lanes), 1)
    per = lanes // ny

    def lane(rows):
        return lane_n if rows == n else lane_w

    def fold(acc, value, y, roll=True):
        moved = pltpu.roll(value, y * per + W, 1) if roll else value
        return jnp.where(lane(value.shape[0]) // per == y, moved, acc)

    def z_near(value, packed, y):
        e = pltpu.roll(packed, lanes - W - y * per, 1)
        ln = lane(value.shape[0])
        up = pltpu.roll(jnp.where(ln == lanes - 1, e, value), 1, 1)
        down = pltpu.roll(jnp.where(ln == 0, e, value), lanes - 1, 1)
        return down, up

    k_w = lane_w % per

    def z_near_packed(packed, own):
        up = pltpu.roll(jnp.where(k_w == W - 1, own, packed), 1, 1)
        down = pltpu.roll(jnp.where(k_w == W, own, packed), lanes - 1, 1)
        return down, up

    def y_near_packed(packed):
        return pltpu.roll(packed, lanes - per, 1), pltpu.roll(packed, per, 1)

    def split_dot(value, weights):
        high = value.astype(bf16)
        low = (value - high.astype(f32)).astype(bf16)
        return jnp.dot(jnp.concatenate([high, low], axis=1), weights, preferred_element_type=f32)

    r2 = lax.broadcasted_iota(jnp.int32, (2 * lanes, lanes), 0) % lanes
    c2 = lax.broadcasted_iota(jnp.int32, (2 * lanes, lanes), 1)
    ones = jnp.ones((2 * lanes, lanes), bf16)
    before = jnp.where(r2 < c2, 1.0, jnp.where(r2 == c2, 0.5, 0.0)).astype(bf16)
    both = jnp.concatenate([before, ones], axis=1)
    kr, kc = r2 % per, c2 % per
    same = (r2 // per) == (c2 // per)
    after_w = jnp.where(kr == kc, 0.5, jnp.where((kr >= W) & (kr < kc), 1.0, 0.0))
    before_w = jnp.where(kr == kc, -0.5, jnp.where((kr < W) & (kr > kc), -1.0, 0.0))
    packed_sum = jnp.where(same, jnp.where(kc >= W, after_w, before_w), 0.0).astype(bf16)

    zslab = jnp.zeros(perm.shape[1:], f32)
    for ref in (perm, ca, cb, pa, pb):
        ref[0] = zslab
        ref[ny + 1] = zslab
    zrows = jnp.zeros((LO, lanes), f32)

    def clear(y, carry):
        for ref in (perm, pa, pb, ca, cb):
            ref[y + 1, 0:LO, :] = zrows
            ref[y + 1, hi_row:hi_row + LO, :] = zrows
        return carry
    yloop(clear, 0)
    cyp[0] = zslab
    cxp[:, 0:LO, :] = jnp.zeros((ny, LO, lanes), f32)
    hf[...] = jnp.zeros_like(hf)

    zn = jnp.zeros((n, lanes), f32)
    center = pl.ds(mid, n)
    window = pl.ds(LO, wide)

    def own_fields(y, carry):
        zp, zt, zs, zc, tot = carry
        mark, t, c = m_in[y], t_in[y], c_in[y]
        liq = jnp.where(mark == 1, 1.0, jnp.where(mark == 2, 0.0, f_in[y]))
        solid = 1.0 - liq
        pm = k_in[y] * (liq * liq * liq / (solid * solid + 0.25) + 0.02)
        sr = 2.0 * liq * solid * t
        perm[y + 1, center, :] = pm
        temp[y, center, :] = t
        srcn[y, center, :] = sr
        ca[y + 1, center, :] = c
        rl[y] = SOLUTE_RATE / (liq + 0.1)
        for f, v in enumerate((pm, t, sr)):
            sxs[0, f, y] = v[0:W]
            sxs[1, f, y] = v[n - W:n]
        xs[0, 0, y] = c[0:W]
        xs[0, 1, y] = c[n - W:n]
        tot_y = split_dot(1.0 + 0.2 * c - 0.3 * t, ones)
        return (fold(zp, pm, y), fold(zt, t, y), fold(zs, sr, y), fold(zc, c, y), fold(tot, tot_y, y, False))

    def post(s, zc, tot):
        r = jnp.where(lane_n % per < W, zc, tot)
        rs[s] = r
        ls[s] = zc
        es[s, 0] = r[0:W]
        es[s, 1] = r[n - W:n]
        fs[s, 0] = zc[0:W]
        fs[s, 1] = zc[n - W:n]
        start(step_copies(s))

    zp, zt, zs, zc, tot = yloop(own_fields, (zn,) * 5)
    for f, v in enumerate((zp, zt, zs)):
        szs[f] = v
        ses[0, f] = v[0:W]
        ses[1, f] = v[n - W:n]
    pl.semaphore_wait(barrier, count)
    start(static_copies())
    post(0, zc, tot)

    top, bottom = pl.ds(LO, W), pl.ds(mid + n, W)
    k_n = lane_n % per
    k_e = lax.broadcasted_iota(jnp.int32, (W, lanes), 1) % per

    arrive(static_copies())
    for f, h in enumerate((PERM, TEMP, SRC)):
        hf[h, center, :] = jnp.where(k_n < W, szr[0, f], szr[1, f])
        hf[h, top, :] = jnp.where(k_e < W, ser[0, 0, f], ser[0, 1, f])
        hf[h, bottom, :] = jnp.where(k_e < W, ser[1, 0, f], ser[1, 1, f])

    def spread(y, carry):
        for f, (ref, o) in enumerate(((perm, 1), (temp, 0), (srcn, 0))):
            ref[y + o, top, :] = sxr[0, f, y]
            ref[y + o, bottom, :] = sxr[1, f, y]
        return carry
    yloop(spread, 0)

    up_rows, down_rows = pl.ds(LO + 1, wide), pl.ds(LO - 1, wide)

    def diagonal_of(pm, near):
        c = [0.5 * (pm + other) for other in near]
        total = c[0] + c[1] + c[2] + c[3] + c[4] + c[5]
        inv = jnp.where(pm > 0.0, 1.0 / jnp.where(pm > 0.0, total, 1.0), 0.0)
        return c, inv

    def coefficients(y, acc):
        pm = perm[y + 1, window, :]
        dz, uz = z_near(pm, hf[PERM, window, :], y)
        c, inv = diagonal_of(pm, [perm[y + 1, up_rows, :], perm[y + 1, down_rows, :],
                                  perm[y + 2, window, :], perm[y, window, :], dz, uz])
        cxp[y, window, :] = c[0]
        cyp[y + 1, window, :] = c[2]

        @pl.when(y == 0)
        def _():
            cyp[0, window, :] = c[3]
        czp[y, window, :] = c[4]
        czm[y, window, :] = c[5]
        for ref, v in zip((axp, axm, ayp, aym, azp, azm), c):
            ref[y] = v * inv
        srcn[y, window, :] = srcn[y, window, :] * inv
        return fold(acc, pm, y)

    zw = jnp.zeros((wide, lanes), f32)
    own = yloop(coefficients, zw)
    pm = hf[PERM, window, :]
    yp, ym = y_near_packed(pm)
    first, last = lane_w < per, lane_w >= lanes - per
    yp, ym = jnp.where(last, 0.0, yp), jnp.where(first, 0.0, ym)
    dz, uz = z_near_packed(pm, own)
    c, inv = diagonal_of(pm, [hf[PERM, up_rows, :], hf[PERM, down_rows, :], yp, ym, dz, uz])
    c[2], c[3] = jnp.where(last, 0.0, c[2]), jnp.where(first, 0.0, c[3])
    for h, v in zip((AXP, AXM, AYP, AYM, AZP, AZM, SRCN), c + [hf[SRC, window, :]]):
        hf[h, window, :] = v * inv

    conc, conc_next = ca, cb
    for s in range(STEPS):
        arrive(step_copies(s))
        hf[CONC, center, :] = jnp.where(k_n < W, rr[s, 0], lr[s])
        hf[CONC, top, :] = jnp.where(k_e < W, er[s, 0, 0], fr[s, 0])
        hf[CONC, bottom, :] = jnp.where(k_e < W, er[s, 1, 0], fr[s, 1])
        total = [rr[s, 0], er[s, 0, 0], er[s, 1, 0]]
        for d in range(1, nz - 1):
            total = [total[0] + rr[s, d], total[1] + er[s, 0, d], total[2] + er[s, 1, d]]
        off[center, :], off[top, :], off[bottom, :] = total
        hpm = hf[PERM, window, :]
        hrho = jnp.where(hpm > 0.0, 1.0 + 0.2 * hf[CONC, window, :] - 0.3 * hf[TEMP, window, :], 0.0)
        hf[RHO, window, :] = hrho

        def head(y, carry, conc=conc, s=s):
            acc, tot = carry
            conc[y + 1, top, :] = xr[s, 0, y]
            conc[y + 1, bottom, :] = xr[s, 1, y]
            real = perm[y + 1, window, :] > 0.0
            rho = jnp.where(real, 1.0 + 0.2 * conc[y + 1, window, :] - 0.3 * temp[y, window, :], 0.0)
            sums = split_dot(rho, both)
            above = pltpu.roll(off[window, :], lanes - W - y * per, 1)[:, 0:1]
            pa[y + 1, window, :] = jnp.where(real, gravity * (above + sums[:, 0:lanes]), 0.0)
            dz, uz = z_near(rho, hf[RHO, window, :], y)
            down, up = half * (rho + dz), half * (rho + uz)
            ld[y, window, :] = down
            lu[y, window, :] = up
            bb[y] = srcn[y, window, :] - azp[y] * down + azm[y] * up
            return fold(acc, rho, y), fold(tot, sums[:, lanes:2 * lanes], y, False)

        own, tot = yloop(head, (zw, zw))
        above = off[window, :]
        above = jnp.where(k_w >= W, above + tot, pltpu.roll(above, lanes - W, 1))
        hf[PH, window, :] = jnp.where(hpm > 0.0, gravity * (above + split_dot(hrho, packed_sum)), 0.0)
        dz, uz = z_near_packed(hrho, own)
        hf[BH, window, :] = hf[SRCN, window, :] - half * (
            hf[AZP, window, :] * (hrho + dz) - hf[AZM, window, :] * (hrho + uz))

        old, new = pa, pb
        for sweep in range(SWEEPS):
            def relax(y, acc, old=old, new=new):
                p = old[y + 1, window, :]
                dz, uz = z_near(p, hf[PH, window, :], y)
                v = bb[y] + axp[y] * old[y + 1, up_rows, :] + axm[y] * old[y + 1, down_rows, :]
                v = v + (ayp[y] * old[y + 2, window, :] + aym[y] * old[y, window, :])
                v = v + (azp[y] * dz + azm[y] * uz)
                new[y + 1, window, :] = v
                return fold(acc, p, y)

            own = yloop(relax, zw)
            p = hf[PH, window, :]
            dz, uz = z_near_packed(p, own)
            yp, ym = y_near_packed(p)
            v = hf[BH, window, :] + hf[AXP, window, :] * hf[PH, up_rows, :] + hf[AXM, window, :] * hf[PH, down_rows, :]
            v = v + hf[AYP, window, :] * yp + hf[AYM, window, :] * ym
            v = v + hf[AZP, window, :] * dz + hf[AZM, window, :] * uz
            hf[PH, window, :] = v
            old, new = new, old

        final = s == STEPS - 1
        up_c, down_c = pl.ds(mid + 1, n), pl.ds(mid - 1, n)

        def transport(y, carry, old=old, conc=conc, conc_next=conc_next, s=s, final=final):
            p, c = old[y + 1, center, :], conc[y + 1, center, :]
            pdz, puz = z_near(p, hf[PH, center, :], y)
            cdz, cuz = z_near(c, hf[CONC, center, :], y)

            def carried(flow, near):
                return flow * jnp.where(flow > 0.0, c, near)

            change = carried(cxp[y, center, :] * (p - old[y + 1, up_c, :]), conc[y + 1, up_c, :])
            change = change + carried(cxp[y, down_c, :] * (p - old[y + 1, down_c, :]), conc[y + 1, down_c, :])
            change = change + carried(cyp[y + 1, center, :] * (p - old[y + 2, center, :]), conc[y + 2, center, :])
            change = change + carried(cyp[y, center, :] * (p - old[y, center, :]), conc[y, center, :])
            change = change + carried(czp[y, center, :] * (p - pdz + ld[y, center, :]), cdz)
            change = change + carried(czm[y, center, :] * (p - puz - lu[y, center, :]), cuz)
            fresh = c - rl[y] * change
            if final:
                p_out[y] = p
                c_out[y] = fresh
                return carry
            zc, tot = carry
            conc_next[y + 1, center, :] = fresh
            xs[s + 1, 0, y] = fresh[0:W]
            xs[s + 1, 1, y] = fresh[n - W:n]
            tot_y = split_dot(1.0 + 0.2 * fresh - 0.3 * t_in[y], ones)
            return fold(zc, fresh, y), fold(tot, tot_y, y, False)

        if final:
            yloop(transport, 0)
        else:
            zc, tot = yloop(transport, (zn, zn))
            post(s + 1, zc, tot)
        conc, conc_next = conc_next, conc

    sent(static_copies())
    for s in range(STEPS):
        sent(step_copies(s))


def on_device(nx, nz, *args):
    ny, n, lanes = args[0].shape
    wide = n + 2 * W
    rows = wide + 2 * LO
    partners = 3 * (nz + 1) - 1

    def vmem(*shape):
        return pltpu.VMEM(shape, jnp.float32)

    padded, layered = (ny + 2, rows, lanes), (ny, rows, lanes)
    scratch = [vmem(*padded), vmem(*layered)] + [vmem(*padded)] * 4
    scratch += [vmem(ny, wide, lanes)] * 6 + [vmem(*layered)]
    scratch += [vmem(*layered), vmem(ny + 1, rows, lanes), vmem(*layered), vmem(*layered),
                vmem(ny, n, lanes), vmem(ny, wide, lanes), vmem(*layered), vmem(*layered)]
    scratch += [vmem(14, rows, lanes), vmem(rows, lanes)]
    scratch += [vmem(STEPS, 2, ny, W, lanes)] * 2
    scratch += [vmem(STEPS, n, lanes), vmem(STEPS, nz - 1, n, lanes)]
    scratch += [vmem(STEPS, 2, W, lanes), vmem(STEPS, 2, nz - 1, W, lanes)]
    scratch += [vmem(STEPS, n, lanes)] * 2 + [vmem(STEPS, 2, W, lanes)] * 2
    scratch += [vmem(2, 3, ny, W, lanes)] * 2
    scratch += [vmem(3, n, lanes), vmem(2, 3, n, lanes), vmem(2, 3, W, lanes), vmem(2, 2, 3, W, lanes)]
    scratch += [pltpu.SemaphoreType.DMA((STEPS, partners))] * 2 + [pltpu.SemaphoreType.DMA((8,))] * 2
    return tuple(pl.pallas_call(
        functools.partial(kernel, nx, nz),
        out_shape=[jax.ShapeDtypeStruct((ny, n, lanes), jnp.float32)] * 2,
        in_specs=[pl.BlockSpec(memory_space=pltpu.VMEM)] * 5,
        out_specs=[pl.BlockSpec(memory_space=pltpu.VMEM)] * 2,
        scratch_shapes=scratch,
        compiler_params=pltpu.CompilerParams(
            collective_id=0, has_side_effects=True, vmem_limit_bytes=40 * 1024 * 1024),
    )(*args))


def solution(mesh):
    placed = P(None, "gx", "gz")
    return jax.shard_map(
        functools.partial(on_device, mesh.shape["gx"], mesh.shape["gz"]),
        mesh=mesh,
        in_specs=(placed,) * 5,
        out_specs=(placed, placed),
        check_vma=False,
    )
```

time: 474 us -> 68.5 us (0.14)
  the two profiles are of different devices: /device:TPU:26 before, /device:TPU:0 now
where the time goes in v1:
time: 68.5 us; the launch traced here: 68.2 us
  Pallas kernels  61.1 us (89%)
  local copies, waits for them, and re-layouts  6.46 us (9%)
    pallas_call x1, Pallas kernels, on_device(): pl.pallas_call(functools.partial(kernel, nx, nz), out_shape=[jax.ShapeDty...  61.1 us
    unnamed x12, local copies, waits for them, and re-layouts  6.46 us

profile of v1, /device:TPU:0, one launch (start us, length us, event | category | flops | bytes accessed | tf_op | source)
XLA Modules:
  0.0 68.2 jit_solution(17472441720228953950)
XLA Ops:
  0.6 0.0 copy-start
  0.6 1.0 %copy-done = f32[16,48,128]{2,1,0:T(8,128)S(1)} copy-done((f32[16,48,128]{2,1,0:T(8,128)S(1)}, f32[16,48,128]{2,1,0:T(8,128)}, u32[]{:S(2)}) %copy-start) | copy-done | bytes 393240
  1.6 0.0 copy-start.1
  1.6 1.0 %copy-done.1 = f32[16,48,128]{2,1,0:T(8,128)S(1)} copy-done((f32[16,48,128]{2,1,0:T(8,128)S(1)}, f32[16,48,128]{2,1,0:T(8,128)}, u32[]{:S(2)}) %copy-start.1) | copy-done | bytes 393240
  2.6 0.0 copy-start.2
  2.6 1.0 %copy-done.2 = f32[16,48,128]{2,1,0:T(8,128)S(1)} copy-done((f32[16,48,128]{2,1,0:T(8,128)S(1)}, f32[16,48,128]{2,1,0:T(8,128)}, u32[]{:S(2)}) %copy-start.2) | copy-done | bytes 393240
  3.6 0.0 copy-start.3
  3.6 1.0 %copy-done.3 = f32[16,48,128]{2,1,0:T(8,128)S(1)} copy-done((f32[16,48,128]{2,1,0:T(8,128)S(1)}, f32[16,48,128]{2,1,0:T(8,128)}, u32[]{:S(2)}) %copy-start.3) | copy-done | bytes 393240
  4.6 0.0 copy-start.4
  4.6 1.0 %copy-done.4 = s32[16,48,128]{2,1,0:T(8,128)S(1)} copy-done((s32[16,48,128]{2,1,0:T(8,128)S(1)}, s32[16,48,128]{2,1,0:T(8,128)}, u32[]{:S(2)}) %copy-start.4) | copy-done | bytes 393240
  5.6 61.1 %shard_map.68 = (f32[16,48,128]{2,1,0:T(8,128)S(1)}, f32[16,48,128]{2,1,0:T(8,128)S(1)}) custom-call(f32[16,48,128]{2,1,0:T(8,128)S(1)} %copy-done, f32[16,48,128]{2,1,0:T(8,128)S(1)} %copy-done.1, f32[16,48,128]{2,1,0:T(8,128)S(1)} %copy-done.2, f32[16,48,128]{2,1,0:T(8,128)S(1)} %copy-done.3, s32[16,48,128]{2,1,0:T(8,128)S(1)} %copy-done.4), custom_call_target="tpu_custom_call" | custom-call | tf_op jit(solution)/shard_map/pallas_call | solution.py:395
  66.7 0.7 %copy.9 = f32[16,48,128]{2,1,0:T(8,128)} copy(f32[16,48,128]{2,1,0:T(8,128)S(1)} %get-tuple-element.4) | data formatting | bytes 786432
  67.5 0.7 %copy.10 = f32[16,48,128]{2,1,0:T(8,128)} copy(f32[16,48,128]{2,1,0:T(8,128)S(1)} %get-tuple-element.5) | data formatting | bytes 786432
Async XLA Ops:
  0.6 1.0 %copy-start = (f32[16,48,128]{2,1,0:T(8,128)S(1)}, f32[16,48,128]{2,1,0:T(8,128)}, u32[]{:S(2)}) copy-start(f32[16,48,128]{2,1,0:T(8,128)} %refs_0_.1) | copy-start | bytes 1179652
  1.6 1.0 %copy-start.1 = (f32[16,48,128]{2,1,0:T(8,128)S(1)}, f32[16,48,128]{2,1,0:T(8,128)}, u32[]{:S(2)}) copy-start(f32[16,48,128]{2,1,0:T(8,128)} %refs_1_.1) | copy-start | bytes 1179652
  2.6 1.0 %copy-start.2 = (f32[16,48,128]{2,1,0:T(8,128)S(1)}, f32[16,48,128]{2,1,0:T(8,128)}, u32[]{:S(2)}) copy-start(f32[16,48,128]{2,1,0:T(8,128)} %refs_2_.1) | copy-start | bytes 1179652
  3.6 1.0 %copy-start.3 = (f32[16,48,128]{2,1,0:T(8,128)S(1)}, f32[16,48,128]{2,1,0:T(8,128)}, u32[]{:S(2)}) copy-start(f32[16,48,128]{2,1,0:T(8,128)} %refs_3_.1) | copy-start | bytes 1179652
  4.6 1.0 %copy-start.4 = (s32[16,48,128]{2,1,0:T(8,128)S(1)}, s32[16,48,128]{2,1,0:T(8,128)}, u32[]{:S(2)}) copy-start(s32[16,48,128]{2,1,0:T(8,128)} %refs_4_.1) | copy-start | bytes 1179652

commit v2 on v1

--- a/solution.py
+++ b/solution.py
@@ -12,22 +12,24 @@
 W = SWEEPS + 1
 SOLUTE_RATE = 0.5
 MESH = pl.DeviceIdType.MESH
-UNROLL = 2
+UNROLL = 4
 
 LO = 8
 
 
 def kernel(nx, nz, *refs):
     it = iter(refs)
-    t_in, c_in, f_in, k_in, m_in, p_out, c_out = [next(it) for _ in range(7)]
+    hbm = [next(it) for _ in range(5)]
+    p_out, c_out = [next(it) for _ in range(2)]
+    t_in, c_in, f_in, k_in, m_in = staged = [next(it) for _ in range(5)]
     perm, temp, ca, cb, pa, pb = [next(it) for _ in range(6)]
     axp, axm, ayp, aym, azp, azm, srcn = [next(it) for _ in range(7)]
     cxp, cyp, czp, czm, rl, bb, ld, lu = [next(it) for _ in range(8)]
     hf = next(it)
-    off = next(it)
-    xs, xr, rs, rr, es, er, ls, lr, fs, fr = [next(it) for _ in range(10)]
+    off, totp, hl, pf, hx, hxt = [next(it) for _ in range(6)]
+    xs, xr, zs, zr, es, er, ts, tr = [next(it) for _ in range(8)]
     sxs, sxr, szs, szr, ses, ser = [next(it) for _ in range(6)]
-    send_sem, recv_sem, st_send, st_recv = [next(it) for _ in range(4)]
+    send_sem, recv_sem, st_send, st_recv, in_sem = [next(it) for _ in range(5)]
 
     ny, n, lanes = t_in.shape
     wide = n + 2 * W
@@ -45,25 +47,22 @@
 
     partners = [(dx, dz) for dz in range(-1, nz) for dx in (-1, 0, 1) if (dx, dz) != (0, 0)]
 
-    def step_copies(s):
-        out = []
+    def step_copies(s, totals):
+        plan = []
         for dx, dz in partners:
             a, b = (1, 0) if dx > 0 else (0, 1)
             if dz == 0:
-                src, dst = xs.at[s, a], xr.at[s, b]
-            elif dz > 0 and dx == 0:
-                src, dst = rs.at[s], rr.at[s, dz - 1]
-            elif dz > 0:
-                src, dst = es.at[s, a], er.at[s, b, dz - 1]
-            elif dx == 0:
-                src, dst = ls.at[s], lr.at[s]
-            else:
-                src, dst = fs.at[s, a], fr.at[s, b]
-            m = len(out)
-            out.append((dx, dz, pltpu.make_async_remote_copy(
-                src_ref=src, dst_ref=dst, send_sem=send_sem.at[s, m], recv_sem=recv_sem.at[s, m],
-                device_id={"gx": ix + dx, "gz": iz + dz}, device_id_type=MESH)))
-        return out
+                plan.append((dx, dz, xs.at[s, a], xr.at[s, b]))
+            elif dz in (-1, 1) and dx == 0:
+                plan.append((dx, dz, zs.at[s], zr.at[s, 0 if dz > 0 else 1]))
+            elif dz in (-1, 1):
+                plan.append((dx, dz, es.at[s, a], er.at[s, b, 0 if dz > 0 else 1]))
+            if dz > 0:
+                plan.append((dx, dz, ts.at[s], tr.at[s, 1 - dx, dz - 1]))
+        return [(dx, dz, pltpu.make_async_remote_copy(
+            src_ref=src, dst_ref=dst, send_sem=send_sem.at[s, m], recv_sem=recv_sem.at[s, m],
+            device_id={"gx": ix + dx, "gz": iz + dz}, device_id_type=MESH))
+            for m, (dx, dz, src, dst) in enumerate(plan) if (dst.shape == (8, lanes)) == totals]
 
     def static_copies():
         out = []
@@ -95,7 +94,11 @@
         for dx, dz, c in copies:
             pl.when(inside(dx, dz))(c.wait_send)
 
-    for ref in (xr, rr, er, lr, fr, sxr, szr, ser):
+    loads = [pltpu.make_async_copy(a, b, in_sem.at[i]) for i, (a, b) in enumerate(zip(hbm, staged))]
+    for load in loads:
+        load.start()
+
+    for ref in (xr, zr, er, tr, sxr, szr, ser):
         ref[...] = jnp.zeros_like(ref)
     barrier = pltpu.get_barrier_semaphore()
     count = 0
@@ -140,10 +143,13 @@
     def y_near_packed(packed):
         return pltpu.roll(packed, lanes - per, 1), pltpu.roll(packed, per, 1)
 
-    def split_dot(value, weights):
+    def split(value):
         high = value.astype(bf16)
         low = (value - high.astype(f32)).astype(bf16)
-        return jnp.dot(jnp.concatenate([high, low], axis=1), weights, preferred_element_type=f32)
+        return jnp.concatenate([high, low], axis=1)
+
+    def split_dot(value, weights):
+        return jnp.dot(split(value), weights, preferred_element_type=f32)
 
     r2 = lax.broadcasted_iota(jnp.int32, (2 * lanes, lanes), 0) % lanes
     c2 = lax.broadcasted_iota(jnp.int32, (2 * lanes, lanes), 1)
@@ -154,6 +160,7 @@
     same = (r2 // per) == (c2 // per)
     after_w = jnp.where(kr == kc, 0.5, jnp.where((kr >= W) & (kr < kc), 1.0, 0.0))
     before_w = jnp.where(kr == kc, -0.5, jnp.where((kr < W) & (kr > kc), -1.0, 0.0))
+    spread_w = jnp.where(same, 1.0, 0.0).astype(bf16)
     packed_sum = jnp.where(same, jnp.where(kc >= W, after_w, before_w), 0.0).astype(bf16)
 
     zslab = jnp.zeros(perm.shape[1:], f32)
@@ -172,12 +179,14 @@
     cxp[:, 0:LO, :] = jnp.zeros((ny, LO, lanes), f32)
     hf[...] = jnp.zeros_like(hf)
 
+    for load in loads:
+        load.wait()
     zn = jnp.zeros((n, lanes), f32)
     center = pl.ds(mid, n)
     window = pl.ds(LO, wide)
 
     def own_fields(y, carry):
-        zp, zt, zs, zc, tot = carry
+        zp, zt, zsr, zc = carry
         mark, t, c = m_in[y], t_in[y], c_in[y]
         liq = jnp.where(mark == 1, 1.0, jnp.where(mark == 2, 0.0, f_in[y]))
         solid = 1.0 - liq
@@ -193,27 +202,37 @@
             sxs[1, f, y] = v[n - W:n]
         xs[0, 0, y] = c[0:W]
         xs[0, 1, y] = c[n - W:n]
-        tot_y = split_dot(1.0 + 0.2 * c - 0.3 * t, ones)
-        return (fold(zp, pm, y), fold(zt, t, y), fold(zs, sr, y), fold(zc, c, y), fold(tot, tot_y, y, False))
-
-    def post(s, zc, tot):
-        r = jnp.where(lane_n % per < W, zc, tot)
-        rs[s] = r
-        ls[s] = zc
-        es[s, 0] = r[0:W]
-        es[s, 1] = r[n - W:n]
-        fs[s, 0] = zc[0:W]
-        fs[s, 1] = zc[n - W:n]
-        start(step_copies(s))
-
-    zp, zt, zs, zc, tot = yloop(own_fields, (zn,) * 5)
-    for f, v in enumerate((zp, zt, zs)):
+        hl[y] = split(1.0 + 0.2 * c - 0.3 * t)
+        return fold(zp, pm, y), fold(zt, t, y), fold(zsr, sr, y), fold(zc, c, y)
+
+    lane_8 = lax.broadcasted_iota(jnp.int32, (8, lanes), 1)
+
+    def post(s, zc):
+        zs[s] = zc
+        es[s, 0] = zc[0:W]
+        es[s, 1] = zc[n - W:n]
+        start(step_copies(s, False))
+        sums = jnp.dot(hl[...].reshape(ny * n, 2 * lanes), both, preferred_element_type=f32)
+        pf[:, center, :] = sums[:, 0:lanes].reshape(ny, n, lanes)
+        totals = sums[:, lanes:2 * lanes].reshape(ny, n, lanes)
+        tot = zn
+        for y in range(ny):
+            tot = jnp.where(lane_n // per == y, totals[y], tot)
+        totp[center, :] = tot
+        packed = jnp.zeros((8, lanes), f32)
+        for j in range(n // 8):
+            packed = jnp.where(lane_8 % per == j, tot[8 * j:8 * j + 8], packed)
+        ts[s] = packed
+        start(step_copies(s, True))
+
+    zp, zt, zsr, zc = yloop(own_fields, (zn,) * 4)
+    for f, v in enumerate((zp, zt, zsr)):
         szs[f] = v
         ses[0, f] = v[0:W]
         ses[1, f] = v[n - W:n]
     pl.semaphore_wait(barrier, count)
     start(static_copies())
-    post(0, zc, tot)
+    post(0, zc)
 
     top, bottom = pl.ds(LO, W), pl.ds(mid + n, W)
     k_n = lane_n % per
@@ -270,39 +289,64 @@
     for h, v in zip((AXP, AXM, AYP, AYM, AZP, AZM, SRCN), c + [hf[SRC, window, :]]):
         hf[h, window, :] = v * inv
 
+    hx[:, 0:W, :] = sxr[0, 1]
+    hx[:, W:2 * W, :] = sxr[1, 1]
+    hxt[...] = hx[...]
+
     conc, conc_next = ca, cb
     for s in range(STEPS):
-        arrive(step_copies(s))
-        hf[CONC, center, :] = jnp.where(k_n < W, rr[s, 0], lr[s])
-        hf[CONC, top, :] = jnp.where(k_e < W, er[s, 0, 0], fr[s, 0])
-        hf[CONC, bottom, :] = jnp.where(k_e < W, er[s, 1, 0], fr[s, 1])
-        total = [rr[s, 0], er[s, 0, 0], er[s, 1, 0]]
-        for d in range(1, nz - 1):
-            total = [total[0] + rr[s, d], total[1] + er[s, 0, d], total[2] + er[s, 1, d]]
-        off[center, :], off[top, :], off[bottom, :] = total
+        arrive(step_copies(s, False))
+        hf[CONC, center, :] = jnp.where(k_n < W, zr[s, 0], zr[s, 1])
+        hf[CONC, top, :] = jnp.where(k_e < W, er[s, 0, 0], er[s, 0, 1])
+        hf[CONC, bottom, :] = jnp.where(k_e < W, er[s, 1, 0], er[s, 1, 1])
+        hx[:, 0:W, :] = xr[s, 0]
+        hx[:, W:2 * W, :] = xr[s, 1]
+        strips = split_dot(1.0 + 0.2 * hx[...].reshape(ny * 2 * W, lanes) - 0.3 * hxt[...].reshape(ny * 2 * W, lanes), both)
+        heads = strips[:, 0:lanes].reshape(ny, 2 * W, lanes)
+        pf[:, top, :] = heads[:, 0:W]
+        pf[:, bottom, :] = heads[:, W:2 * W]
+        tails = strips[:, lanes:2 * lanes].reshape(ny, 2 * W, lanes)
+        tot = jnp.zeros((2 * W, lanes), f32)
+        for y in range(ny):
+            tot = jnp.where(lane_8 // per == y, tails[y], tot)
+        totp[top, :] = tot[0:W]
+        totp[bottom, :] = tot[W:2 * W]
         hpm = hf[PERM, window, :]
         hrho = jnp.where(hpm > 0.0, 1.0 + 0.2 * hf[CONC, window, :] - 0.3 * hf[TEMP, window, :], 0.0)
         hf[RHO, window, :] = hrho
 
-        def head(y, carry, conc=conc, s=s):
-            acc, tot = carry
+        def head(y, acc, conc=conc, s=s):
             conc[y + 1, top, :] = xr[s, 0, y]
             conc[y + 1, bottom, :] = xr[s, 1, y]
             real = perm[y + 1, window, :] > 0.0
             rho = jnp.where(real, 1.0 + 0.2 * conc[y + 1, window, :] - 0.3 * temp[y, window, :], 0.0)
-            sums = split_dot(rho, both)
-            above = pltpu.roll(off[window, :], lanes - W - y * per, 1)[:, 0:1]
-            pa[y + 1, window, :] = jnp.where(real, gravity * (above + sums[:, 0:lanes]), 0.0)
+            pa[y + 1, window, :] = jnp.where(real, gravity * pf[y, window, :], 0.0)
             dz, uz = z_near(rho, hf[RHO, window, :], y)
             down, up = half * (rho + dz), half * (rho + uz)
             ld[y, window, :] = down
             lu[y, window, :] = up
             bb[y] = srcn[y, window, :] - azp[y] * down + azm[y] * up
-            return fold(acc, rho, y), fold(tot, sums[:, lanes:2 * lanes], y, False)
-
-        own, tot = yloop(head, (zw, zw))
+            return fold(acc, rho, y)
+
+        own = yloop(head, zw)
+        arrive(step_copies(s, True))
+        total = [tr[s, side, 0] for side in range(3)]
+        for d in range(1, nz - 1):
+            total = [total[side] + tr[s, side, d] for side in range(3)]
+        for j in range(n // 8):
+            off[pl.ds(mid + 8 * j, 8), :] = jnp.where(lane_8 % per == j, total[1], 0.0)
+        off[top, :] = jnp.where(lane_8 % per == n // 8 - 1, total[0], 0.0)[8 - W:8]
+        off[bottom, :] = jnp.where(lane_8 % per == 0, total[2], 0.0)[0:W]
+        off[window, :] = split_dot(off[window, :], spread_w)
+
+        def lower(y, carry):
+            real = perm[y + 1, window, :] > 0.0
+            above = pltpu.roll(off[window, :], lanes - W - y * per, 1)[:, 0:1]
+            pa[y + 1, window, :] = pa[y + 1, window, :] + jnp.where(real, gravity * above, 0.0)
+            return carry
+        yloop(lower, 0)
         above = off[window, :]
-        above = jnp.where(k_w >= W, above + tot, pltpu.roll(above, lanes - W, 1))
+        above = jnp.where(k_w >= W, above + totp[window, :], above)
         hf[PH, window, :] = jnp.where(hpm > 0.0, gravity * (above + split_dot(hrho, packed_sum)), 0.0)
         dz, uz = z_near_packed(hrho, own)
         hf[BH, window, :] = hf[SRCN, window, :] - half * (
@@ -332,7 +376,7 @@
         final = s == STEPS - 1
         up_c, down_c = pl.ds(mid + 1, n), pl.ds(mid - 1, n)
 
-        def transport(y, carry, old=old, conc=conc, conc_next=conc_next, s=s, final=final):
+        def transport(y, zc, old=old, conc=conc, conc_next=conc_next, s=s, final=final):
             p, c = old[y + 1, center, :], conc[y + 1, center, :]
             pdz, puz = z_near(p, hf[PH, center, :], y)
             cdz, cuz = z_near(c, hf[CONC, center, :], y)
@@ -350,56 +394,58 @@
             if final:
                 p_out[y] = p
                 c_out[y] = fresh
-                return carry
-            zc, tot = carry
+                return zc
             conc_next[y + 1, center, :] = fresh
             xs[s + 1, 0, y] = fresh[0:W]
             xs[s + 1, 1, y] = fresh[n - W:n]
-            tot_y = split_dot(1.0 + 0.2 * fresh - 0.3 * t_in[y], ones)
-            return fold(zc, fresh, y), fold(tot, tot_y, y, False)
+            hl[y] = split(1.0 + 0.2 * fresh - 0.3 * t_in[y])
+            return fold(zc, fresh, y)
 
         if final:
             yloop(transport, 0)
         else:
-            zc, tot = yloop(transport, (zn, zn))
-            post(s + 1, zc, tot)
+            post(s + 1, yloop(transport, zn))
         conc, conc_next = conc_next, conc
 
     sent(static_copies())
     for s in range(STEPS):
-        sent(step_copies(s))
+        sent(step_copies(s, False))
+        sent(step_copies(s, True))
 
 
 def on_device(nx, nz, *args):
     ny, n, lanes = args[0].shape
     wide = n + 2 * W
     rows = wide + 2 * LO
-    partners = 3 * (nz + 1) - 1
+    copies = 2 + 6 + 3 * (nz - 1)
 
     def vmem(*shape):
         return pltpu.VMEM(shape, jnp.float32)
 
     padded, layered = (ny + 2, rows, lanes), (ny, rows, lanes)
-    scratch = [vmem(*padded), vmem(*layered)] + [vmem(*padded)] * 4
+    scratch = [pltpu.VMEM((ny, n, lanes), a.dtype) for a in args]
+    scratch += [vmem(*padded), vmem(*layered)] + [vmem(*padded)] * 4
     scratch += [vmem(ny, wide, lanes)] * 6 + [vmem(*layered)]
     scratch += [vmem(*layered), vmem(ny + 1, rows, lanes), vmem(*layered), vmem(*layered),
                 vmem(ny, n, lanes), vmem(ny, wide, lanes), vmem(*layered), vmem(*layered)]
-    scratch += [vmem(14, rows, lanes), vmem(rows, lanes)]
+    scratch += [vmem(14, rows, lanes), vmem(rows, lanes), vmem(rows, lanes)]
+    scratch += [pltpu.VMEM((ny, n, 2 * lanes), jnp.bfloat16), vmem(*layered)] + [vmem(ny, 2 * W, lanes)] * 2
     scratch += [vmem(STEPS, 2, ny, W, lanes)] * 2
-    scratch += [vmem(STEPS, n, lanes), vmem(STEPS, nz - 1, n, lanes)]
-    scratch += [vmem(STEPS, 2, W, lanes), vmem(STEPS, 2, nz - 1, W, lanes)]
-    scratch += [vmem(STEPS, n, lanes)] * 2 + [vmem(STEPS, 2, W, lanes)] * 2
+    scratch += [vmem(STEPS, n, lanes), vmem(STEPS, 2, n, lanes)]
+    scratch += [vmem(STEPS, 2, W, lanes), vmem(STEPS, 2, 2, W, lanes)]
+    scratch += [vmem(STEPS, 8, lanes), vmem(STEPS, 3, nz - 1, 8, lanes)]
     scratch += [vmem(2, 3, ny, W, lanes)] * 2
     scratch += [vmem(3, n, lanes), vmem(2, 3, n, lanes), vmem(2, 3, W, lanes), vmem(2, 2, 3, W, lanes)]
-    scratch += [pltpu.SemaphoreType.DMA((STEPS, partners))] * 2 + [pltpu.SemaphoreType.DMA((8,))] * 2
+    scratch += [pltpu.SemaphoreType.DMA((STEPS, copies))] * 2 + [pltpu.SemaphoreType.DMA((8,))] * 2
+    scratch += [pltpu.SemaphoreType.DMA((5,))]
     return tuple(pl.pallas_call(
         functools.partial(kernel, nx, nz),
         out_shape=[jax.ShapeDtypeStruct((ny, n, lanes), jnp.float32)] * 2,
-        in_specs=[pl.BlockSpec(memory_space=pltpu.VMEM)] * 5,
+        in_specs=[pl.BlockSpec(memory_space=pltpu.HBM)] * 5,
         out_specs=[pl.BlockSpec(memory_space=pltpu.VMEM)] * 2,
         scratch_shapes=scratch,
         compiler_params=pltpu.CompilerParams(
-            collective_id=0, has_side_effects=True, vmem_limit_bytes=40 * 1024 * 1024),
+            collective_id=0, has_side_effects=True, vmem_limit_bytes=63 * 1024 * 1024),
     )(*args))
 
 

time: 68.5 us -> 58 us (0.85)
  Pallas kernels: 61.1 us -> 54.6 us
  local copies, waits for them, and re-layouts: 6.46 us -> 2.57 us
    pallas_call x1, Pallas kernels: 61.1 us -> 54.6 us  [on_device(): pl.pallas_call(functools.partial(kernel, nx, nz), out_shape=[jax.ShapeDty...]
    unnamed x12 -> x4, local copies, waits for them, and re-layouts: 6.46 us -> 2.57 us
where the time goes in v2:
time: 58 us; the launch traced here: 57.8 us
  Pallas kernels  54.6 us (94%)
  local copies, waits for them, and re-layouts  2.57 us (4%)
  between operations  0.65 us (1%)
    pallas_call x1, Pallas kernels, on_device(): pl.pallas_call(functools.partial(kernel, nx, nz), out_shape=[jax.ShapeDty...  54.6 us
    unnamed x4, local copies, waits for them, and re-layouts  2.57 us

profile of v2, /device:TPU:0, one launch (start us, length us, event | category | flops | bytes accessed | tf_op | source)
XLA Modules:
  0.0 57.8 jit_solution(6562821058915152434)
XLA Ops:
  0.6 54.6 %shard_map.68 = (f32[16,48,128]{2,1,0:T(8,128)}, f32[16,48,128]{2,1,0:T(8,128)}) custom-call(f32[16,48,128]{2,1,0:T(8,128)} %refs_0_.1, f32[16,48,128]{2,1,0:T(8,128)} %refs_1_.1, f32[16,48,128]{2,1,0:T(8,128)} %refs_2_.1, f32[16,48,128]{2,1,0:T(8,128)} %refs_3_.1, s32[16,48,128]{2,1,0:T(8,128)} %refs_4_.1), custom_call_target="tpu_custom_call" | custom-call | tf_op jit(solution)/shard_map/pallas_call | solution.py:441
  55.2 0.0 copy-start
  55.2 1.8 %copy.9 = f32[16,48,128]{2,1,0:T(8,128)} copy(f32[16,48,128]{2,1,0:T(8,128)} %get-tuple-element.4) | data formatting | bytes 786432
  57.0 0.0 copy-done
  57.0 0.7 %copy.10 = f32[16,48,128]{2,1,0:T(8,128)} copy(f32[16,48,128]{2,1,0:T(8,128)S(1)} %copy-done) | data formatting | bytes 786432
Async XLA Ops:
  55.2 1.8 %copy-start = (f32[16,48,128]{2,1,0:T(8,128)S(1)}, f32[16,48,128]{2,1,0:T(8,128)}, u32[]{:S(2)}) copy-start(f32[16,48,128]{2,1,0:T(8,128)} %get-tuple-element.5) | copy-start | bytes 1179652

commit v3 on v2

--- a/solution.py
+++ b/solution.py
@@ -108,12 +108,12 @@
             pl.semaphore_signal(barrier, inc=1, device_id={"gx": ix - dx, "gz": iz - dz}, device_id_type=MESH)
         count = count + inside(dx, dz).astype(jnp.int32)
 
-    def yloop(body, init):
+    def yloop(body, init, unroll=UNROLL):
         def group(g, carry):
-            for u in range(UNROLL):
-                carry = body(g * UNROLL + u, carry)
+            for u in range(unroll):
+                carry = body(g * unroll + u, carry)
             return carry
-        return lax.fori_loop(0, ny // UNROLL, group, init)
+        return lax.fori_loop(0, ny // unroll, group, init)
 
     lane_n = lax.broadcasted_iota(jnp.int32, (n, lanes), 1)
     lane_w = lax.broadcasted_iota(jnp.int32, (wide, lanes), 1)
@@ -363,7 +363,7 @@
                 new[y + 1, window, :] = v
                 return fold(acc, p, y)
 
-            own = yloop(relax, zw)
+            own = yloop(relax, zw, 8)
             p = hf[PH, window, :]
             dz, uz = z_near_packed(p, own)
             yp, ym = y_near_packed(p)

time: 58 us -> 60.7 us (1.047)
  Pallas kernels: 54.6 us -> 57.3 us
    pallas_call x1, Pallas kernels: 54.6 us -> 57.3 us  [on_device(): pl.pallas_call(functools.partial(kernel, nx, nz), out_shape=[jax.ShapeDty...]
where the time goes in v3:
time: 60.7 us; the launch traced here: 60.6 us
  Pallas kernels  57.3 us (94%)
  local copies, waits for them, and re-layouts  2.57 us (4%)
  between operations  0.65 us (1%)
    pallas_call x1, Pallas kernels, on_device(): pl.pallas_call(functools.partial(kernel, nx, nz), out_shape=[jax.ShapeDty...  57.3 us
    unnamed x4, local copies, waits for them, and re-layouts  2.57 us

profile of v3, /device:TPU:0, one launch (start us, length us, event | category | flops | bytes accessed | tf_op | source)
XLA Modules:
  0.0 60.6 jit_solution(3894483853220161136)
XLA Ops:
  0.6 57.3 %shard_map.68 = (f32[16,48,128]{2,1,0:T(8,128)}, f32[16,48,128]{2,1,0:T(8,128)}) custom-call(f32[16,48,128]{2,1,0:T(8,128)} %refs_0_.1, f32[16,48,128]{2,1,0:T(8,128)} %refs_1_.1, f32[16,48,128]{2,1,0:T(8,128)} %refs_2_.1, f32[16,48,128]{2,1,0:T(8,128)} %refs_3_.1, s32[16,48,128]{2,1,0:T(8,128)} %refs_4_.1), custom_call_target="tpu_custom_call" | custom-call | tf_op jit(solution)/shard_map/pallas_call | solution.py:441
  58.0 0.0 copy-start
  58.0 1.8 %copy.9 = f32[16,48,128]{2,1,0:T(8,128)} copy(f32[16,48,128]{2,1,0:T(8,128)} %get-tuple-element.4) | data formatting | bytes 786432
  59.8 0.0 copy-done
  59.8 0.7 %copy.10 = f32[16,48,128]{2,1,0:T(8,128)} copy(f32[16,48,128]{2,1,0:T(8,128)S(1)} %copy-done) | data formatting | bytes 786432
Async XLA Ops:
  58.0 1.8 %copy-start = (f32[16,48,128]{2,1,0:T(8,128)S(1)}, f32[16,48,128]{2,1,0:T(8,128)}, u32[]{:S(2)}) copy-start(f32[16,48,128]{2,1,0:T(8,128)} %get-tuple-element.5) | copy-start | bytes 1179652
